TPU v7x, 32 devices: a whole 2x2x4 slice. The times are simulated.
32 devices in a mesh: grp: 2 (over x), seq: 16 (over z, y, core).
Axes of the slice: x: 2, y: 2, z: 4, core: 2. Of those that a mesh axis runs over, the one named last changes fastest.
Arguments:
- frames: bfloat16 [4096, 2048], P(('grp', 'seq')), parts along dimension 0
- conv_weight: bfloat16 [4, 2048], replicated, may hold values from -2.390625 to 2.390625
- qkv_weight: bfloat16 [2048, 3072], P(None, 'seq'), may hold values from -0.125 to 0.125
- track_ids: int32 [4096], P(('grp', 'seq')), parts along dimension 0, may hold values from 0 to 63, as said below
- track_owner: int32 [128], P('grp'), parts along dimension 0, may hold values from 0 to 15, as said below
Outputs:
- context: bfloat16 [4096, 1024], P(('grp', 'seq')), parts along dimension 0
There are 2 independent parts, one for each index of `grp`. A program takes and returns all parts, laid end to end along the dimension named above; an argument that names none is the same for every part. Nothing has to cross between parts.
Inputs may be any that keep to these rules, and one draw needn't show every extreme that they name: `track_ids`: counting each token by track_owner of its track, the tokens of one device fall on each owning device at most 16 times, and one owning device receives exactly 16 tokens from every device. `track_owner`: every device owns exactly 4 tracks.
All inputs are finite; a program needn't handle non-finite values.
Results may differ from a plain program's by a relative error of at most 0.005.
The roundings to bfloat16 on the way count: a program that leaves them out, or rounds other values in their place, can miss the bound.
Values may be sent and summed in bfloat16 or wider, within the bound.
No kernel may reach another device: no remote copies, remote signals or barrier semaphores. Data moves between devices by JAX's collectives and lax.ppermute only.
A program may use at most 64 MiB of HBM per device.

v0:
```python
import jax
import jax.numpy as jnp
from jax import lax
from jax.experimental import pallas as pl
from jax.experimental.pallas import tpu as pltpu
from jax.sharding import Mesh
from jax.sharding import PartitionSpec as P

HD = 128
KW = 4


def from_behind(value, axis, by):
    size = lax.axis_size(axis)
    pairs = [(i, i + by) for i in range(size) if 0 <= i + by < size]
    return lax.ppermute(value, axis, pairs)


def track_groups(track_ids, track_owner):
    track_total = track_owner.shape[0]
    return jnp.sum(
        jnp.where(
            track_ids[:, None] == jnp.arange(track_total, dtype=jnp.int32)[None, :],
            track_owner[None, :],
            0,
        ),
        axis=1,
    )


def convolve(frames, conv_weight, rim_rows):
    tok_rows = frames.shape[0]
    extended = jnp.concatenate([rim_rows, frames], axis=0).astype(jnp.float32)
    conv_sum = frames.astype(jnp.float32)
    for tap in range(KW):
        conv_sum = (
            conv_sum
            + conv_weight[tap].astype(jnp.float32)[None, :]
            * extended[KW - 1 - tap : KW - 1 - tap + tok_rows]
        )
    return conv_sum.astype(jnp.bfloat16)


def attend_slots(packed, positions):
    slot_count = packed.shape[0]
    inner = packed.shape[1] // 3
    head_count = inner // HD
    query = packed[:, :inner].reshape(slot_count, head_count, HD)
    keys_all = packed[:, inner : 2 * inner].reshape(slot_count, head_count, HD)
    values_all = packed[:, 2 * inner :].reshape(slot_count, head_count, HD)
    slot_ids = jnp.arange(slot_count, dtype=jnp.int32)
    score_scale = 1.0 / HD**0.5
    scores = (
        jnp.einsum("qhd,khd->hqk", query, keys_all, preferred_element_type=jnp.float32)
        * score_scale
    )
    allowed = (positions[None, :] >= 0) & (positions[None, :] <= positions[:, None]) | (
        slot_ids[:, None] == slot_ids[None, :]
    )
    scores = jnp.where(allowed[None], scores, jnp.float32(-1e30))
    top_score = jnp.max(scores, axis=-1, keepdims=True)
    expd = jnp.exp(scores - top_score)
    weights = (expd / jnp.sum(expd, axis=-1, keepdims=True)).astype(jnp.bfloat16)
    mixed = jnp.einsum("hqk,khd->qhd", weights, values_all, preferred_element_type=jnp.float32)
    return mixed.astype(jnp.bfloat16).reshape(slot_count, inner)


def body_by_owner(frames, conv_weight, qkv_weight, track_ids, track_owner):
    tok_rows = frames.shape[0]
    peer_count = lax.axis_size("seq")
    capacity = 2 * tok_rows // peer_count
    slot_total = capacity * peer_count
    my_index = lax.axis_index("seq")
    rim_rows = from_behind(frames[tok_rows - (KW - 1) :], "seq", 1)
    hidden = convolve(frames, conv_weight, rim_rows)
    group = track_groups(track_ids, track_owner)
    owner_hits = (group[:, None] == jnp.arange(peer_count, dtype=jnp.int32)[None, :]).astype(
        jnp.int32
    )
    running = jnp.cumsum(owner_hits, axis=0) - 1
    rank_rows = jnp.sum(jnp.where(owner_hits > 0, running, 0), axis=1)
    slot_of_row = group * capacity + rank_rows
    row_ids = jnp.arange(tok_rows, dtype=jnp.int32)
    source_row = jnp.full((slot_total,), tok_rows, jnp.int32).at[slot_of_row].set(row_ids)
    positions = my_index * tok_rows + row_ids
    send_times = jnp.full((slot_total,), -1, jnp.int32).at[slot_of_row].set(positions)
    projected = jnp.dot(
        hidden,
        lax.all_gather(qkv_weight, "seq", axis=1, tiled=True),
        preferred_element_type=jnp.float32,
    ).astype(jnp.bfloat16)
    padded_rows = jnp.concatenate(
        [projected, jnp.zeros((1, projected.shape[1]), jnp.bfloat16)], axis=0
    )
    outgoing = padded_rows[source_row]
    received, got_times = (
        lax.all_to_all(outgoing, "seq", split_axis=0, concat_axis=0, tiled=True),
        lax.all_to_all(send_times, "seq", split_axis=0, concat_axis=0, tiled=True),
    )
    mixed = attend_slots(received, got_times)
    returned = lax.all_to_all(mixed, "seq", split_axis=0, concat_axis=0, tiled=True)
    return returned[slot_of_row]


FOUR = ("far", "near", "quad")
CORE, Y, NEAR, FAR = 1, 2, 4, 8
RIM = 16


def swap_seq(value, bit):
    count = lax.axis_size(FOUR)
    return lax.ppermute(value, FOUR, [(d, d ^ bit) for d in range(count)])


def swap_grp(value):
    return lax.ppermute(value, "grp", [(0, 1), (1, 0)])


def call(kernel, out_shape, operands, name, smem=0, flops=0, limit=6):
    whole = pl.BlockSpec()
    scalars = pl.BlockSpec(memory_space=pltpu.SMEM)
    many = isinstance(out_shape, (list, tuple))
    shapes = list(out_shape) if many else [out_shape]
    return pl.pallas_call(
        kernel,
        out_shape=out_shape,
        in_specs=[scalars] * smem + [whole] * (len(operands) - smem),
        out_specs=[whole] * len(shapes) if many else whole,
        cost_estimate=pl.CostEstimate(
            flops=flops,
            bytes_accessed=sum(2 * o.size for o in list(operands) + shapes),
            transcendentals=0,
        ),
        compiler_params=pltpu.CompilerParams(vmem_limit_bytes=limit * 2**20),
        name=name,
    )(*operands)


def bf16(*shape):
    return jax.ShapeDtypeStruct(shape, jnp.bfloat16)


def after_kernel(*refs):
    del refs


def after(value, *others):
    anywhere = pl.BlockSpec(memory_space=pl.ANY)
    return pl.pallas_call(
        after_kernel,
        out_shape=jax.ShapeDtypeStruct(value.shape, value.dtype),
        in_specs=[anywhere] * (1 + len(others)),
        out_specs=anywhere,
        input_output_aliases={0: 0},
        compiler_params=pltpu.CompilerParams(vmem_limit_bytes=2**20),
        name="after",
    )(value, *others)


def convolved(before, rows, taps):
    count = rows.shape[0]
    rows = rows.astype(jnp.float32)
    extended = jnp.concatenate([before.astype(jnp.float32), rows], axis=0)
    taps = taps.astype(jnp.float32)
    total = rows
    for tap in range(KW):
        total = total + taps[tap : tap + 1] * extended[RIM - tap : RIM - tap + count]
    return total.astype(jnp.bfloat16)


ME, SIDE, GRP, TURN, TURN_PAIRED, HEAD, DEVICES = range(7)


def code_kernel(scalars, owner, ids, code):
    group = jnp.zeros(ids.shape, jnp.int32)
    for track in range(owner.shape[0]):
        group = jnp.where(ids[...] == track, owner[track], group)
    time = lax.broadcasted_iota(jnp.int32, ids.shape, 1)
    code[...] = (group * scalars[DEVICES] + scalars[ME]) * ids.shape[1] + time


def first_kernel(
    scalars, frames, weight, taps, late, rim, block0, block1, block2, rows, tap_rows, sems
):
    tok_rows = frames.shape[0]
    part = late.shape[0]
    half = block0.shape[1]
    lanes = pl.ds(pl.multiple_of(scalars[GRP] * half, half), half)
    copies = [
        pltpu.make_async_copy(frames, rows, sems.at[0]),
        pltpu.make_async_copy(taps, tap_rows, sems.at[1]),
    ]
    for j, block in enumerate((block0, block1, block2)):
        source = weight.at[pl.ds(j * (HD // 2), HD // 2), lanes]
        copies.append(pltpu.make_async_copy(source, block, sems.at[2 + j]))
    for copy in copies:
        copy.start()
    copies[0].wait()
    copies[1].wait()
    late[...] = convolved(rows[part - RIM : part], rows[part:], tap_rows[...])
    rim[...] = rows[tok_rows - RIM :]
    for copy in copies[2:]:
        copy.wait()


def first(scalars, frames, weight, taps):
    tok_rows, features = frames.shape
    half = features // 2
    whole, anywhere = pl.BlockSpec(), pl.BlockSpec(memory_space=pl.ANY)
    return pl.pallas_call(
        first_kernel,
        out_shape=[bf16(tok_rows // 2, features), bf16(RIM, features)]
        + [bf16(HD // 2, half)] * 3,
        in_specs=[pl.BlockSpec(memory_space=pltpu.SMEM)] + [anywhere] * 3,
        out_specs=[whole] * 5,
        scratch_shapes=[
            pltpu.VMEM(frames.shape, frames.dtype),
            pltpu.VMEM(taps.shape, taps.dtype),
            pltpu.SemaphoreType.DMA((5,)),
        ],
        compiler_params=pltpu.CompilerParams(vmem_limit_bytes=48 * 2**20),
        name="first",
    )(scalars, frames, weight, taps)


def early_kernel(rim, frames, taps, late, early, own):
    part = late.shape[0]
    rows = convolved(rim[...], frames[:part], taps[...])
    early[...] = rows
    own[:part] = rows
    own[part:] = late[...]


def assemble_kernel(scalars, mine, mine_too, paired, diagonal0, diagonal1, weight):
    side, grp = scalars[SIDE], scalars[GRP]
    half, cut = mine.shape[2], diagonal0.shape[2]
    for piece, column, start, turn in (
        (mine, side, grp * half, TURN),
        (mine_too, side, (1 - grp) * half, TURN),
        (paired, 1 - side, grp * half, TURN_PAIRED),
        (diagonal0, 1 - side, (1 - grp) * half, TURN_PAIRED),
        (diagonal1, 1 - side, (1 - grp) * half + cut, TURN_PAIRED),
    ):
        lanes = pl.ds(pl.multiple_of(start, cut), piece.shape[2])
        for j in range(3):
            at = lax.rem(j + 3 - scalars[turn], 3) * HD + column * (HD // 2)
            weight[pl.ds(pl.multiple_of(at, HD // 2), HD // 2), lanes] = piece[j]


def place_kernel(scalars, block0, block1, block2, block3, theirs, out):
    rows = out.shape[0]
    for n, block in enumerate((block0, block1, block2, block3)):
        chip = (0, Y, FAR, FAR | Y)[n]
        for core, value in ((0, block[...]), (CORE, theirs[n * rows : (n + 1) * rows])):
            head = scalars[HEAD] ^ (chip // FAR * 4 + chip % 4 + core)
            out[:, pl.ds(pl.multiple_of(head * HD, HD), HD)] = value


def body_by_head(frames, conv_weight, qkv_weight, track_ids, track_owner):
    tok_rows, features = frames.shape
    grp = lax.axis_index("grp")
    far, near, quad = (lax.axis_index(name) for name in FOUR)
    me = far * FAR + near * NEAR + quad
    devices = lax.axis_size(FOUR)
    head = far * 4 + quad
    part = tok_rows // 2

    half = features // 2
    turn = lax.rem(2 * head + near, 3)
    turn_paired = lax.rem(2 * head + 1 - near, 3)
    scalars = jnp.stack([me, near, grp, turn, turn_paired, head, devices])
    scalars = scalars.astype(jnp.int32)

    codes = call(
        code_kernel,
        jax.ShapeDtypeStruct((1, tok_rows), jnp.int32),
        [scalars, track_owner, track_ids[None, :]],
        "code",
        smem=2,
        limit=1,
    )
    seen = [0]

    def with_codes_of(codes, bit):
        seen.extend([hop ^ bit for hop in seen])
        return jnp.concatenate([codes, swap_seq(codes, bit)], axis=0)

    codes = with_codes_of(with_codes_of(codes, FAR), NEAR)
    late, rim_rows, *blocks = first(scalars, frames, qkv_weight.T, conv_weight)
    late = after(late, codes)
    rim_rows = after(rim_rows, codes)

    def home(block):
        of_head, side = block % devices // 2, block % 2
        return of_head // 4 * FAR + side * NEAR + of_head % 4

    mine = jnp.stack(
        [
            lax.ppermute(block, FOUR, [(d, home(3 * d + j)) for d in range(devices)])
            for j, block in enumerate(blocks)
        ]
    )
    far_late = swap_seq(late, FAR)
    mine = after(mine, far_late)
    mine_too = swap_grp(mine)
    paired = swap_seq(mine, NEAR)
    cut = half // 2
    diagonal = [swap_grp(paired[:, :, :cut]), swap_seq(mine_too[:, :, cut:], NEAR)]
    head_weight = call(
        assemble_kernel,
        bf16(3 * HD, features),
        [scalars, mine, mine_too, paired] + diagonal,
        "assemble",
        smem=1,
    )

    rim_rows = lax.ppermute(rim_rows, FOUR, [(i, i + 1) for i in range(devices - 1)])
    early, own = call(
        early_kernel,
        [bf16(part, features), bf16(tok_rows, features)],
        [rim_rows, frames, conv_weight, late],
        "early",
    )
    beside = swap_seq(after(own, mine), Y)
    far_late_beside = swap_seq(far_late, Y)
    far_early = swap_seq(after(early, far_late), FAR)
    far_early_beside = swap_seq(after(far_early, *diagonal), Y)

    parts = []

    def project(*rows):
        rows = jnp.concatenate(rows + tuple(swap_seq(r, CORE) for r in rows), axis=0)
        done = lax.dot_general(
            rows, head_weight, (((1,), (1,)), ((), ())), preferred_element_type=jnp.float32
        ).astype(jnp.bfloat16)
        parts.append((done[:, :HD], done[:, HD:], swap_seq(done[:, HD:], NEAR)))
        return done

    done = project(own, beside, far_late, far_late_beside)
    done = project(far_early, after(far_early_beside, done))

    codes = with_codes_of(with_codes_of(after(codes, done), CORE), Y)

    keyed = jnp.concatenate([p[1] for p in parts] + [p[2] for p in parts], axis=0)

    first_order, second_order = [], []
    for core in (0, CORE):
        first_order += [(core, 0, tok_rows), (core | Y, 0, tok_rows)]
        first_order += [(core | FAR, part, part), (core | FAR | Y, part, part)]
        second_order += [(core | FAR, 0, part), (core | FAR | Y, 0, part)]
    order = first_order + second_order

    def codes_at(order, bit=0):
        return jnp.concatenate(
            [codes[seen.index(hop ^ bit), start : start + count] for hop, start, count in order]
        )

    keys = jnp.concatenate([codes_at(order), codes_at(order, NEAR)])
    queries = jnp.concatenate([p[0] for p in parts], axis=0)
    span = devices * tok_rows

    def attend(hops):
        at, pieces = 0, {}
        for hop, start, count in order:
            pieces[hop, start] = queries[at : at + count]
            at += count
        mine = [(h, s, c) for hop in hops for h, s, c in sorted(order) if h == hop]
        query = jnp.concatenate([pieces[h, s] for h, s, _ in mine], axis=0)
        asking = codes_at(mine)
        least = asking // span * span
        scores = lax.dot_general(
            query, keyed[:, :HD], (((1,), (1,)), ((), ())), preferred_element_type=jnp.float32
        ) * (1.0 / HD**0.5)
        allowed = (keys[None, :] <= asking[:, None]) & (keys[None, :] >= least[:, None])
        scores = jnp.where(allowed, scores, jnp.float32(-1e30))
        expd = jnp.exp(scores - jnp.max(scores, axis=-1, keepdims=True))
        weights = (expd / jnp.sum(expd, axis=-1, keepdims=True)).astype(jnp.bfloat16)
        mixed = jnp.dot(weights, keyed[:, HD:], preferred_element_type=jnp.float32)
        return mixed.astype(jnp.bfloat16).reshape(len(hops), tok_rows, HD)

    far_hops = (FAR, FAR | CORE, FAR | Y, FAR | Y | CORE)
    context = attend(far_hops)
    home = {FAR: swap_seq(context[:2], FAR), FAR | Y: swap_seq(context[2:], FAR | Y)}
    context = attend((0, CORE, Y, Y | CORE))
    home[Y] = swap_seq(context[2:], Y)
    home[0] = context[:2]
    chips = (0, Y, FAR, FAR | Y)
    theirs = swap_seq(jnp.concatenate([home[chip][1] for chip in chips], axis=0), CORE)
    return call(
        place_kernel,
        bf16(tok_rows, devices // 2 * HD),
        [scalars] + [home[chip][0] for chip in chips] + [theirs],
        "place",
        smem=1,
    )


def solution(mesh):
    grp, seq = mesh.devices.shape
    out_by_owner = P(("grp", "seq"), None)
    by_owner = jax.shard_map(
        body_by_owner,
        mesh=mesh,
        in_specs=(P(("grp", "seq"), None), P(), P(None, "seq"), P(("grp", "seq")), P("grp")),
        out_specs=out_by_owner,
        check_vma=False,
    )
    fits = (grp, seq) == (2, 16)
    if fits:
        split = Mesh(mesh.devices.reshape(grp, 2, 2, 4), ("grp",) + FOUR)
        rows = P(("grp",) + FOUR)
        by_head = jax.shard_map(
            body_by_head,
            mesh=split,
            in_specs=(rows, P(), P(None, FOUR), rows, P("grp")),
            out_specs=rows,
            check_vma=False,
        )

    def run(frames, conv_weight, qkv_weight, track_ids, track_owner):
        heads = qkv_weight.shape[1] // (3 * HD)
        plan = by_head if fits and heads == 8 else by_owner
        return plan(frames, conv_weight, qkv_weight, track_ids, track_owner)

    return run
```

profile of v0, /device:TPU:0, one launch (start us, length us, event | category | flops | bytes accessed | tf_op | source)
XLA Modules:
  0.0 103.0 jit_solution(10941686133733154916)
XLA Ops:
  2.0 4.1 %collective-permute-start = (s32[1,128]{1,0:T(1,128)S(1)}, s32[1,128]{1,0:T(1,128)S(1)}, u32[]{:S(2)}, u32[]{:S(2)}) collective-permute-start(s32[1,128]{1,0:T(1,128)S(1)} %code.1), channel_id=1, source_target_pairs={{0,8},{1,9},{2,10},{3,11},{4,12},{5,13},{6,14},{7,15},{8,0},{9,1},... | collective-permute-start | bytes 1544 | tf_op jit(solution)/shard_map/ppermute | solution.py:112
  6.1 1.5 %collective-permute-done = s32[1,128]{1,0:T(1,128)S(1)} collective-permute-done((s32[1,128]{1,0:T(1,128)S(1)}, s32[1,128]{1,0:T(1,128)S(1)}, u32[]{:S(2)}, u32[]{:S(2)}) %collective-permute-start) | collective-permute-done | bytes 544 | tf_op jit(solution)/shard_map/ppermute | solution.py:112
  7.6 1.9 %collective-permute-start.1 = (s32[2,128]{1,0:T(2,128)S(1)}, s32[2,128]{1,0:T(2,128)S(1)}, u32[]{:S(2)}, u32[]{:S(2)}) collective-permute-start(s32[2,128]{1,0:T(2,128)S(1)} %pad_add_fusion.3), channel_id=1, source_target_pairs={{0,4},{1,5},{2,6},{3,7},{4,0},{5,1},{6,2},{7,3},{8,12},{9,13},{10,... | collective-permute-start | bytes 3080 | tf_op jit(solution)/shard_map/ppermute | solution.py:112
  16.1 2.7 %collective-permute-start.15 = (bf16[128,2048]{1,0:T(8,128)(2,1)S(1)}, bf16[128,2048]{1,0:T(8,128)(2,1)S(1)}, u32[]{:S(2)}, u32[]{:S(2)}) collective-permute-start(bf16[128,2048]{1,0:T(8,128)(2,1)S(1)} %get-tuple-element.18.refs_0_), channel_id=1, source_target_pairs={{0,1},{1,0},{2,3},{3,2},{4,5},{5,4},{6,7},{7,6},{8,9},{9,8},{10,11... | collective-permute-start | bytes 1572872 | tf_op jit(solution)/shard_map/ppermute | solution.py:112
  18.8 4.3 %collective-permute-start.3 = (bf16[64,2048]{1,0:T(8,128)(2,1)S(1)}, bf16[64,2048]{1,0:T(8,128)(2,1)S(1)}, u32[]{:S(2)}, u32[]{:S(2)}) collective-permute-start(bf16[64,2048]{1,0:T(8,128)(2,1)S(1)} %after.9.late), channel_id=1, source_target_pairs={{0,8},{1,9},{2,10},{3,11},{4,12},{5,13},{6,14},{7,15},{8,0},{9,1},... | collective-permute-start | bytes 786440 | tf_op jit(solution)/shard_map/ppermute | solution.py:112
  23.1 2.1 %collective-permute-start.7 = (bf16[64,1024]{1,0:T(8,128)(2,1)S(1)}, bf16[64,1024]{1,0:T(8,128)(2,1)S(1)}, u32[]{:S(2)}, u32[]{:S(2)}) collective-permute-start(bf16[64,1024]{1,0:T(8,128)(2,1)S(1)} %get-tuple-element.17), channel_id=1, source_target_pairs={{0,1},{1,6},{2,8},{3,13},{4,11},{5,4},{6,2},{7,7},{8,9},{9,14},{10... | collective-permute-start | bytes 393224 | tf_op jit(solution)/shard_map/ppermute | solution.py:299
  25.9 5.5 %collective-permute-start.6 = (bf16[64,1024]{1,0:T(8,128)(2,1)S(1)}, bf16[64,1024]{1,0:T(8,128)(2,1)S(1)}, u32[]{:S(2)}, u32[]{:S(2)}) collective-permute-start(bf16[64,1024]{1,0:T(8,128)(2,1)S(1)} %get-tuple-element.16), channel_id=1, source_target_pairs={{0,4},{1,2},{2,7},{3,9},{4,14},{5,0},{6,5},{7,3},{8,12},{9,10},{10... | collective-permute-start | bytes 393224 | tf_op jit(solution)/shard_map/ppermute | solution.py:299
  31.4 7.1 %collective-permute-done.7 = bf16[64,1024]{1,0:T(8,128)(2,1)S(1)} collective-permute-done((bf16[64,1024]{1,0:T(8,128)(2,1)S(1)}, bf16[64,1024]{1,0:T(8,128)(2,1)S(1)}, u32[]{:S(2)}, u32[]{:S(2)}) %collective-permute-start.7) | collective-permute-done | bytes 131104 | tf_op jit(solution)/shard_map/ppermute | solution.py:299
  38.6 2.6 %collective-permute-done.3.refs_1_ = bf16[64,2048]{1,0:T(8,128)(2,1)S(1)} collective-permute-done((bf16[64,2048]{1,0:T(8,128)(2,1)S(1)}, bf16[64,2048]{1,0:T(8,128)(2,1)S(1)}, u32[]{:S(2)}, u32[]{:S(2)}) %collective-permute-start.3) | collective-permute-done | bytes 262176 | tf_op jit(solution)/shard_map/ppermute | solution.py:112
  41.2 1.6 %collective-permute-start.10 = (bf16[3,64,1024]{2,1,0:T(8,128)(2,1)S(1)}, bf16[3,64,1024]{2,1,0:T(8,128)(2,1)S(1)}, u32[]{:S(2)}, u32[]{:S(2)}) collective-permute-start(bf16[3,64,1024]{2,1,0:T(8,128)(2,1)S(1)} %after.11.refs_1_.mine), channel_id=1, source_target_pairs={{0,16},{16,0},{1,17},{17,1},{2,18},{18,2},{3,19},{19,3},{4,20},{20... | collective-permute-start | bytes 1179656 | tf_op jit(solution)/shard_map/ppermute | solution.py:116
  43.2 4.4 %collective-permute-start.4 = (bf16[64,2048]{1,0:T(8,128)(2,1)S(1)}, bf16[64,2048]{1,0:T(8,128)(2,1)S(1)}, u32[]{:S(2)}, u32[]{:S(2)}) collective-permute-start(bf16[64,2048]{1,0:T(8,128)(2,1)S(1)} %after.10), channel_id=1, source_target_pairs={{0,8},{1,9},{2,10},{3,11},{4,12},{5,13},{6,14},{7,15},{8,0},{9,1},... | collective-permute-start | bytes 786440 | tf_op jit(solution)/shard_map/ppermute | solution.py:112
  47.8 4.5 %collective-permute-done.10.mine_too = bf16[3,64,1024]{2,1,0:T(8,128)(2,1)S(1)} collective-permute-done((bf16[3,64,1024]{2,1,0:T(8,128)(2,1)S(1)}, bf16[3,64,1024]{2,1,0:T(8,128)(2,1)S(1)}, u32[]{:S(2)}, u32[]{:S(2)}) %collective-permute-start.10) | collective-permute-done | bytes 393248 | tf_op jit(solution)/shard_map/ppermute | solution.py:116
  52.4 8.0 %collective-permute-done.8.paired = bf16[3,64,1024]{2,1,0:T(8,128)(2,1)S(1)} collective-permute-done((bf16[3,64,1024]{2,1,0:T(8,128)(2,1)S(1)}, bf16[3,64,1024]{2,1,0:T(8,128)(2,1)S(1)}, u32[]{:S(2)}, u32[]{:S(2)}) %collective-permute-start.8) | collective-permute-done | bytes 393248 | tf_op jit(solution)/shard_map/ppermute | solution.py:112
  63.4 2.7 %collective-permute-done.9.refs_1_.diagonal0 = bf16[3,64,512]{2,1,0:T(8,128)(2,1)S(1)} collective-permute-done((bf16[3,64,512]{2,1,0:T(8,128)(2,1)S(1)}, bf16[3,64,512]{2,1,0:T(8,128)(2,1)S(1)}, u32[]{:S(2)}, u32[]{:S(2)}) %collective-permute-start.9) | collective-permute-done | bytes 196640 | tf_op jit(solution)/shard_map/ppermute | solution.py:116
  67.0 1.8 %collective-permute-done.16 = bf16[128,2048]{1,0:T(8,128)(2,1)S(1)} collective-permute-done((bf16[128,2048]{1,0:T(8,128)(2,1)S(1)}, bf16[128,2048]{1,0:T(8,128)(2,1)S(1)}, u32[]{:S(2)}, u32[]{:S(2)}) %collective-permute-start.16) | collective-permute-done | bytes 524320 | tf_op jit(solution)/shard_map/ppermute | solution.py:112
  68.9 1.8 %convolution_convert_fusion.refs_1_ = bf16[768,384]{1,0:T(8,128)(2,1)S(1)} fusion(bf16[768,2048]{1,0:T(8,128)(2,1)S(1)} %constant_dynamic-update-slice_fusion, bf16[384,2048]{1,0:T(8,128)(2,1)S(1)} %assemble.1), kind=kOutput, calls=%fused_computation.10 | convolution fusion | flops 1208254464 | bytes 5308416 | tf_op jit(solution)/shard_map/dot_general | solution.py:333
  70.7 1.7 %collective-permute-done.12.refs_0_ = bf16[64,2048]{1,0:T(8,128)(2,1)S(1)} collective-permute-done((bf16[64,2048]{1,0:T(8,128)(2,1)S(1)}, bf16[64,2048]{1,0:T(8,128)(2,1)S(1)}, u32[]{:S(2)}, u32[]{:S(2)}) %collective-permute-start.12) | collective-permute-done | bytes 262176 | tf_op jit(solution)/shard_map/ppermute | solution.py:112
  76.5 3.2 %collective-permute-done.22 = s32[8,128]{1,0:T(8,128)S(1)} collective-permute-done((s32[8,128]{1,0:T(8,128)S(1)}, s32[8,128]{1,0:T(8,128)S(1)}, u32[]{:S(2)}, u32[]{:S(2)}) %collective-permute-start.22) | collective-permute-done | bytes 4128 | tf_op jit(solution)/shard_map/ppermute | solution.py:112
  79.9 7.0 %collective-permute-done.24 = bf16[256,256]{1,0:T(8,128)(2,1)S(1)} collective-permute-done((bf16[256,256]{1,0:T(8,128)(2,1)S(1)}, bf16[256,256]{1,0:T(8,128)(2,1)S(1)}, u32[]{:S(2)}, u32[]{:S(2)}) %collective-permute-start.24) | collective-permute-done | bytes 131104 | tf_op jit(solution)/shard_map/ppermute | solution.py:112
  93.2 2.4 %collective-permute-start.27 = (bf16[2,128,128]{2,1,0:T(8,128)(2,1)S(1)}, bf16[2,128,128]{2,1,0:T(8,128)(2,1)S(1)}, u32[]{:S(2)}, u32[]{:S(2)}) collective-permute-start(bf16[2,128,128]{2,1,0:T(8,128)(2,1)S(1)} %bitcast.84), channel_id=1, source_target_pairs={{0,10},{1,11},{2,8},{3,9},{4,14},{5,15},{6,12},{7,13},{8,2},{9,3},... | collective-permute-start | bytes 196616 | tf_op jit(solution)/shard_map/ppermute | solution.py:112
  95.6 1.7 %collective-permute-start.25 = (bf16[2,128,128]{2,1,0:T(8,128)(2,1)S(1)}, bf16[2,128,128]{2,1,0:T(8,128)(2,1)S(1)}, u32[]{:S(2)}, u32[]{:S(2)}) collective-permute-start(bf16[2,128,128]{2,1,0:T(8,128)(2,1)S(1)} %bitcast.83), channel_id=1, source_target_pairs={{0,2},{1,3},{2,0},{3,1},{4,6},{5,7},{6,4},{7,5},{8,10},{9,11},{10,... | collective-permute-start | bytes 196616 | tf_op jit(solution)/shard_map/ppermute | solution.py:112
  97.3 2.2 %collective-permute-done.27 = bf16[2,128,128]{2,1,0:T(8,128)(2,1)S(1)} collective-permute-done((bf16[2,128,128]{2,1,0:T(8,128)(2,1)S(1)}, bf16[2,128,128]{2,1,0:T(8,128)(2,1)S(1)}, u32[]{:S(2)}, u32[]{:S(2)}) %collective-permute-start.27) | collective-permute-done | bytes 65568 | tf_op jit(solution)/shard_map/ppermute | solution.py:112
  100.3 1.3 %collective-permute-done.28.theirs = bf16[512,128]{1,0:T(8,128)(2,1)S(1)} collective-permute-done((bf16[512,128]{1,0:T(8,128)(2,1)S(1)}, bf16[512,128]{1,0:T(8,128)(2,1)S(1)}, u32[]{:S(2)}, u32[]{:S(2)}) %collective-permute-start.28) | collective-permute-done | bytes 131104 | tf_op jit(solution)/shard_map/ppermute | solution.py:112
  101.6 1.3 %place.1 = bf16[128,1024]{1,0:T(8,128)(2,1)} custom-call(s32[7]{0:T(128)S(1)} %stack.39.scalars, bf16[128,128]{1,0:T(8,128)(2,1)S(1)} %get-tuple-element.24.block0, bf16[128,128]{1,0:T(8,128)(2,1)S(1)} %get-tuple-element.28.block1, bf16[128,128]{1,0:T(8,128)(2,1)S(1)} %get-tuple-element.30.block2, bf16[128,128]{1,0:T(8,128)(2,1)S(1)} %get-tuple-element.32.block3, ...), custom_call_target="tpu_custom_call" | custom-call | bytes 524302 | tf_op jit(solution)/shard_map/place/pallas_call | solution.py:124
  (110 shorter events, 25.1 us)
Async XLA Ops:
  2.0 5.6 %collective-permute-start = (s32[1,128]{1,0:T(1,128)S(1)}, s32[1,128]{1,0:T(1,128)S(1)}, u32[]{:S(2)}, u32[]{:S(2)}) collective-permute-start(s32[1,128]{1,0:T(1,128)S(1)} %code.1), channel_id=1, source_target_pairs={{0,8},{1,9},{2,10},{3,11},{4,12},{5,13},{6,14},{7,15},{8,0},{9,1},... | collective-permute-start | bytes 1544 | tf_op jit(solution)/shard_map/ppermute | solution.py:112
  7.6 5.9 %collective-permute-start.1 = (s32[2,128]{1,0:T(2,128)S(1)}, s32[2,128]{1,0:T(2,128)S(1)}, u32[]{:S(2)}, u32[]{:S(2)}) collective-permute-start(s32[2,128]{1,0:T(2,128)S(1)} %pad_add_fusion.3), channel_id=1, source_target_pairs={{0,4},{1,5},{2,6},{3,7},{4,0},{5,1},{6,2},{7,3},{8,12},{9,13},{10,... | collective-permute-start | bytes 3080 | tf_op jit(solution)/shard_map/ppermute | solution.py:112
  16.1 26.7 %collective-permute-start.15 = (bf16[128,2048]{1,0:T(8,128)(2,1)S(1)}, bf16[128,2048]{1,0:T(8,128)(2,1)S(1)}, u32[]{:S(2)}, u32[]{:S(2)}) collective-permute-start(bf16[128,2048]{1,0:T(8,128)(2,1)S(1)} %get-tuple-element.18.refs_0_), channel_id=1, source_target_pairs={{0,1},{1,0},{2,3},{3,2},{4,5},{5,4},{6,7},{7,6},{8,9},{9,8},{10,11... | collective-permute-start | bytes 1572872 | tf_op jit(solution)/shard_map/ppermute | solution.py:112
  18.8 22.3 %collective-permute-start.3 = (bf16[64,2048]{1,0:T(8,128)(2,1)S(1)}, bf16[64,2048]{1,0:T(8,128)(2,1)S(1)}, u32[]{:S(2)}, u32[]{:S(2)}) collective-permute-start(bf16[64,2048]{1,0:T(8,128)(2,1)S(1)} %after.9.late), channel_id=1, source_target_pairs={{0,8},{1,9},{2,10},{3,11},{4,12},{5,13},{6,14},{7,15},{8,0},{9,1},... | collective-permute-start | bytes 786440 | tf_op jit(solution)/shard_map/ppermute | solution.py:112
  23.1 15.4 %collective-permute-start.7 = (bf16[64,1024]{1,0:T(8,128)(2,1)S(1)}, bf16[64,1024]{1,0:T(8,128)(2,1)S(1)}, u32[]{:S(2)}, u32[]{:S(2)}) collective-permute-start(bf16[64,1024]{1,0:T(8,128)(2,1)S(1)} %get-tuple-element.17), channel_id=1, source_target_pairs={{0,1},{1,6},{2,8},{3,13},{4,11},{5,4},{6,2},{7,7},{8,9},{9,14},{10... | collective-permute-start | bytes 393224 | tf_op jit(solution)/shard_map/ppermute | solution.py:299
  25.2 13.3 %collective-permute-start.5 = (bf16[64,1024]{1,0:T(8,128)(2,1)S(1)}, bf16[64,1024]{1,0:T(8,128)(2,1)S(1)}, u32[]{:S(2)}, u32[]{:S(2)}) collective-permute-start(bf16[64,1024]{1,0:T(8,128)(2,1)S(1)} %get-tuple-element.15), channel_id=1, source_target_pairs={{0,0},{1,5},{2,3},{3,12},{4,10},{5,15},{6,1},{7,6},{8,8},{9,13},{1... | collective-permute-start | bytes 393224 | tf_op jit(solution)/shard_map/ppermute | solution.py:299
  25.9 12.7 %collective-permute-start.6 = (bf16[64,1024]{1,0:T(8,128)(2,1)S(1)}, bf16[64,1024]{1,0:T(8,128)(2,1)S(1)}, u32[]{:S(2)}, u32[]{:S(2)}) collective-permute-start(bf16[64,1024]{1,0:T(8,128)(2,1)S(1)} %get-tuple-element.16), channel_id=1, source_target_pairs={{0,4},{1,2},{2,7},{3,9},{4,14},{5,0},{6,5},{7,3},{8,12},{9,10},{10... | collective-permute-start | bytes 393224 | tf_op jit(solution)/shard_map/ppermute | solution.py:299
  41.2 11.1 %collective-permute-start.10 = (bf16[3,64,1024]{2,1,0:T(8,128)(2,1)S(1)}, bf16[3,64,1024]{2,1,0:T(8,128)(2,1)S(1)}, u32[]{:S(2)}, u32[]{:S(2)}) collective-permute-start(bf16[3,64,1024]{2,1,0:T(8,128)(2,1)S(1)} %after.11.refs_1_.mine), channel_id=1, source_target_pairs={{0,16},{16,0},{1,17},{17,1},{2,18},{18,2},{3,19},{19,3},{4,20},{20... | collective-permute-start | bytes 1179656 | tf_op jit(solution)/shard_map/ppermute | solution.py:116
  42.7 17.6 %collective-permute-start.8 = (bf16[3,64,1024]{2,1,0:T(8,128)(2,1)S(1)}, bf16[3,64,1024]{2,1,0:T(8,128)(2,1)S(1)}, u32[]{:S(2)}, u32[]{:S(2)}) collective-permute-start(bf16[3,64,1024]{2,1,0:T(8,128)(2,1)S(1)} %after.11.refs_1_.mine), channel_id=1, source_target_pairs={{0,4},{1,5},{2,6},{3,7},{4,0},{5,1},{6,2},{7,3},{8,12},{9,13},{10,... | collective-permute-start | bytes 1179656 | tf_op jit(solution)/shard_map/ppermute | solution.py:112
  42.8 24.0 %collective-permute-start.13 = (bf16[128,2048]{1,0:T(8,128)(2,1)S(1)}, bf16[128,2048]{1,0:T(8,128)(2,1)S(1)}, u32[]{:S(2)}, u32[]{:S(2)}) collective-permute-start(bf16[128,2048]{1,0:T(8,128)(2,1)S(1)} %after.13), channel_id=1, source_target_pairs={{0,2},{1,3},{2,0},{3,1},{4,6},{5,7},{6,4},{7,5},{8,10},{9,11},{10,... | collective-permute-start | bytes 1572872 | tf_op jit(solution)/shard_map/ppermute | solution.py:112
  43.2 17.7 %collective-permute-start.4 = (bf16[64,2048]{1,0:T(8,128)(2,1)S(1)}, bf16[64,2048]{1,0:T(8,128)(2,1)S(1)}, u32[]{:S(2)}, u32[]{:S(2)}) collective-permute-start(bf16[64,2048]{1,0:T(8,128)(2,1)S(1)} %after.10), channel_id=1, source_target_pairs={{0,8},{1,9},{2,10},{3,11},{4,12},{5,13},{6,14},{7,15},{8,0},{9,1},... | collective-permute-start | bytes 786440 | tf_op jit(solution)/shard_map/ppermute | solution.py:112
  47.7 14.4 %collective-permute-start.14 = (bf16[64,2048]{1,0:T(8,128)(2,1)S(1)}, bf16[64,2048]{1,0:T(8,128)(2,1)S(1)}, u32[]{:S(2)}, u32[]{:S(2)}) collective-permute-start(bf16[64,2048]{1,0:T(8,128)(2,1)S(1)} %collective-permute-done.3.refs_1_), channel_id=1, source_target_pairs={{0,2},{1,3},{2,0},{3,1},{4,6},{5,7},{6,4},{7,5},{8,10},{9,11},{10,... | collective-permute-start | bytes 786440 | tf_op jit(solution)/shard_map/ppermute | solution.py:112
  52.3 11.1 %collective-permute-start.11 = (bf16[3,64,512]{2,1,0:T(8,128)(2,1)S(1)}, bf16[3,64,512]{2,1,0:T(8,128)(2,1)S(1)}, u32[]{:S(2)}, u32[]{:S(2)}) collective-permute-start(bf16[3,64,512]{2,1,0:T(8,128)(2,1)S(1)} %slice.261), channel_id=1, source_target_pairs={{0,4},{1,5},{2,6},{3,7},{4,0},{5,1},{6,2},{7,3},{8,12},{9,13},{10,... | collective-permute-start | bytes 589832 | tf_op jit(solution)/shard_map/ppermute | solution.py:112
  60.4 5.7 %collective-permute-start.9 = (bf16[3,64,512]{2,1,0:T(8,128)(2,1)S(1)}, bf16[3,64,512]{2,1,0:T(8,128)(2,1)S(1)}, u32[]{:S(2)}, u32[]{:S(2)}) collective-permute-start(bf16[3,64,512]{2,1,0:T(8,128)(2,1)S(1)} %slice.260), channel_id=1, source_target_pairs={{0,16},{16,0},{1,17},{17,1},{2,18},{18,2},{3,19},{19,3},{4,20},{20... | collective-permute-start | bytes 589832 | tf_op jit(solution)/shard_map/ppermute | solution.py:116
  60.9 7.9 %collective-permute-start.17 = (bf16[64,2048]{1,0:T(8,128)(2,1)S(1)}, bf16[64,2048]{1,0:T(8,128)(2,1)S(1)}, u32[]{:S(2)}, u32[]{:S(2)}) collective-permute-start(bf16[64,2048]{1,0:T(8,128)(2,1)S(1)} %collective-permute-done.3.refs_1_), channel_id=1, source_target_pairs={{0,1},{1,0},{2,3},{3,2},{4,5},{5,4},{6,7},{7,6},{8,9},{9,8},{10,11... | collective-permute-start | bytes 786440 | tf_op jit(solution)/shard_map/ppermute | solution.py:112
  62.1 10.7 %collective-permute-start.19 = (bf16[64,2048]{1,0:T(8,128)(2,1)S(1)}, bf16[64,2048]{1,0:T(8,128)(2,1)S(1)}, u32[]{:S(2)}, u32[]{:S(2)}) collective-permute-start(bf16[64,2048]{1,0:T(8,128)(2,1)S(1)} %collective-permute-done.4), channel_id=1, source_target_pairs={{0,1},{1,0},{2,3},{3,2},{4,5},{5,4},{6,7},{7,6},{8,9},{9,8},{10,11... | collective-permute-start | bytes 786440 | tf_op jit(solution)/shard_map/ppermute | solution.py:112
  63.4 5.5 %collective-permute-start.18 = (bf16[64,2048]{1,0:T(8,128)(2,1)S(1)}, bf16[64,2048]{1,0:T(8,128)(2,1)S(1)}, u32[]{:S(2)}, u32[]{:S(2)}) collective-permute-start(bf16[64,2048]{1,0:T(8,128)(2,1)S(1)} %collective-permute-done.14), channel_id=1, source_target_pairs={{0,1},{1,0},{2,3},{3,2},{4,5},{5,4},{6,7},{7,6},{8,9},{9,8},{10,11... | collective-permute-start | bytes 786440 | tf_op jit(solution)/shard_map/ppermute | solution.py:112
  66.1 6.4 %collective-permute-start.12 = (bf16[64,2048]{1,0:T(8,128)(2,1)S(1)}, bf16[64,2048]{1,0:T(8,128)(2,1)S(1)}, u32[]{:S(2)}, u32[]{:S(2)}) collective-permute-start(bf16[64,2048]{1,0:T(8,128)(2,1)S(1)} %after.12), channel_id=1, source_target_pairs={{0,2},{1,3},{2,0},{3,1},{4,6},{5,7},{6,4},{7,5},{8,10},{9,11},{10,... | collective-permute-start | bytes 786440 | tf_op jit(solution)/shard_map/ppermute | solution.py:112
  72.5 14.4 %collective-permute-start.23 = (bf16[768,256]{1,0:T(8,128)(2,1)S(1)}, bf16[768,256]{1,0:T(8,128)(2,1)S(1)}, u32[]{:S(2)}, u32[]{:S(2)}) collective-permute-start(bf16[768,256]{1,0:T(8,128)(2,1)S(1)} %slice.266), channel_id=1, source_target_pairs={{0,4},{1,5},{2,6},{3,7},{4,0},{5,1},{6,2},{7,3},{8,12},{9,13},{10,... | collective-permute-start | bytes 1179656 | tf_op jit(solution)/shard_map/ppermute | solution.py:112
  75.1 11.8 %collective-permute-start.24 = (bf16[256,256]{1,0:T(8,128)(2,1)S(1)}, bf16[256,256]{1,0:T(8,128)(2,1)S(1)}, u32[]{:S(2)}, u32[]{:S(2)}) collective-permute-start(bf16[256,256]{1,0:T(8,128)(2,1)S(1)} %slice.267), channel_id=1, source_target_pairs={{0,4},{1,5},{2,6},{3,7},{4,0},{5,1},{6,2},{7,3},{8,12},{9,13},{10,... | collective-permute-start | bytes 393224 | tf_op jit(solution)/shard_map/ppermute | solution.py:112
  76.0 3.6 %collective-permute-start.22 = (s32[8,128]{1,0:T(8,128)S(1)}, s32[8,128]{1,0:T(8,128)S(1)}, u32[]{:S(2)}, u32[]{:S(2)}) collective-permute-start(s32[8,128]{1,0:T(8,128)S(1)} %pad_add_fusion), channel_id=1, source_target_pairs={{0,2},{1,3},{2,0},{3,1},{4,6},{5,7},{6,4},{7,5},{8,10},{9,11},{10,... | collective-permute-start | bytes 12296 | tf_op jit(solution)/shard_map/ppermute | solution.py:112
  89.9 7.4 %collective-permute-start.26 = (bf16[2,128,128]{2,1,0:T(8,128)(2,1)S(1)}, bf16[2,128,128]{2,1,0:T(8,128)(2,1)S(1)}, u32[]{:S(2)}, u32[]{:S(2)}) collective-permute-start(bf16[2,128,128]{2,1,0:T(8,128)(2,1)S(1)} %bitcast.85), channel_id=1, source_target_pairs={{0,8},{1,9},{2,10},{3,11},{4,12},{5,13},{6,14},{7,15},{8,0},{9,1},... | collective-permute-start | bytes 196616 | tf_op jit(solution)/shard_map/ppermute | solution.py:112
  93.2 6.3 %collective-permute-start.27 = (bf16[2,128,128]{2,1,0:T(8,128)(2,1)S(1)}, bf16[2,128,128]{2,1,0:T(8,128)(2,1)S(1)}, u32[]{:S(2)}, u32[]{:S(2)}) collective-permute-start(bf16[2,128,128]{2,1,0:T(8,128)(2,1)S(1)} %bitcast.84), channel_id=1, source_target_pairs={{0,10},{1,11},{2,8},{3,9},{4,14},{5,15},{6,12},{7,13},{8,2},{9,3},... | collective-permute-start | bytes 196616 | tf_op jit(solution)/shard_map/ppermute | solution.py:112
  95.6 4.6 %collective-permute-start.25 = (bf16[2,128,128]{2,1,0:T(8,128)(2,1)S(1)}, bf16[2,128,128]{2,1,0:T(8,128)(2,1)S(1)}, u32[]{:S(2)}, u32[]{:S(2)}) collective-permute-start(bf16[2,128,128]{2,1,0:T(8,128)(2,1)S(1)} %bitcast.83), channel_id=1, source_target_pairs={{0,2},{1,3},{2,0},{3,1},{4,6},{5,7},{6,4},{7,5},{8,10},{9,11},{10,... | collective-permute-start | bytes 196616 | tf_op jit(solution)/shard_map/ppermute | solution.py:112
  (10 other events, 12.5 us)
where the time goes:
time: 103 us
  waiting for transfers between devices  49 us (48%)
  starting transfers between devices  36.1 us (35%)
  matrix products  6.83 us (7%)
  local copies, waits for them, and re-layouts  5.12 us (5%)
  Pallas kernels  4.02 us (4%)
  other arithmetic  1.6 us (2%)
    ppermute x23, waiting for transfers between devices, swap_seq(): return lax.ppermute(value, FOUR, [(d, d ^ bit) for d in range(count)])  33.7 us
    ppermute x23, starting transfers between devices, swap_seq(): return lax.ppermute(value, FOUR, [(d, d ^ bit) for d in range(count)])  24.4 us
    ppermute x3, starting transfers between devices, body_by_head(): lax.ppermute(block, FOUR, [(d, home(3 * d + j)) for d in range(devices)])  8.25 us
    ppermute x2, waiting for transfers between devices, swap_grp(): return lax.ppermute(value, 'grp', [(0, 1), (1, 0)])  7.22 us
    ppermute x3, waiting for transfers between devices, body_by_head(): lax.ppermute(block, FOUR, [(d, home(3 * d + j)) for d in range(devices)])  7.15 us
    unnamed x25, local copies, waits for them, and re-layouts  4.48 us
    pallas_call x4, Pallas kernels, call(): pl.pallas_call(kernel, out_shape=out_shape, in_specs=[scalars] * smem + [...  2.94 us
    dot_general x2, matrix products, attend(): lax.dot_general(query, keyed[:, :HD], (((1,), (1,)), ((), ())), preferred...  2.54 us
  transfers between devices with their start and end apart: 29, of which 17 were waited for; matrix products, arithmetic and copies ran while one was open for 6% of the time, Pallas kernels for 2%

commit v1 on v0

--- a/solution.py
+++ b/solution.py
@@ -168,19 +168,12 @@
     return total.astype(jnp.bfloat16)
 
 
-ME, SIDE, GRP, TURN, TURN_PAIRED, HEAD, DEVICES = range(7)
-
-
-def code_kernel(scalars, owner, ids, code):
-    group = jnp.zeros(ids.shape, jnp.int32)
-    for track in range(owner.shape[0]):
-        group = jnp.where(ids[...] == track, owner[track], group)
-    time = lax.broadcasted_iota(jnp.int32, ids.shape, 1)
-    code[...] = (group * scalars[DEVICES] + scalars[ME]) * ids.shape[1] + time
+ME, SIDE, GRP, TURN, TURN_PAIRED, HEAD = range(6)
 
 
 def first_kernel(
-    scalars, frames, weight, taps, late, rim, block0, block1, block2, rows, tap_rows, sems
+    scalars, owner, ids, frames, weight, taps, late, rim, block0, block1, block2, code,
+    rows, tap_rows, my_ids, owners, sems,
 ):
     tok_rows = frames.shape[0]
     part = late.shape[0]
@@ -189,38 +182,48 @@
     copies = [
         pltpu.make_async_copy(frames, rows, sems.at[0]),
         pltpu.make_async_copy(taps, tap_rows, sems.at[1]),
+        pltpu.make_async_copy(ids, my_ids, sems.at[2]),
+        pltpu.make_async_copy(owner, owners, sems.at[3]),
     ]
     for j, block in enumerate((block0, block1, block2)):
         source = weight.at[pl.ds(j * (HD // 2), HD // 2), lanes]
-        copies.append(pltpu.make_async_copy(source, block, sems.at[2 + j]))
+        copies.append(pltpu.make_async_copy(source, block, sems.at[4 + j]))
     for copy in copies:
         copy.start()
-    copies[0].wait()
-    copies[1].wait()
+    for copy in copies[:4]:
+        copy.wait()
     late[...] = convolved(rows[part - RIM : part], rows[part:], tap_rows[...])
     rim[...] = rows[tok_rows - RIM :]
-    for copy in copies[2:]:
+    group = jnp.zeros(ids.shape, jnp.int32)
+    for track in range(owner.shape[1]):
+        group = jnp.where(my_ids[...] == track, owners[0, track], group)
+    time = lax.broadcasted_iota(jnp.int32, ids.shape, 1)
+    code[...] = (group * 16 + scalars[ME]) * tok_rows + time
+    for copy in copies[4:]:
         copy.wait()
 
 
-def first(scalars, frames, weight, taps):
+def first(scalars, owner, ids, frames, weight, taps):
     tok_rows, features = frames.shape
     half = features // 2
-    whole, anywhere = pl.BlockSpec(), pl.BlockSpec(memory_space=pl.ANY)
+    whole, far = pl.BlockSpec(), pl.BlockSpec(memory_space=pltpu.HBM)
     return pl.pallas_call(
         first_kernel,
         out_shape=[bf16(tok_rows // 2, features), bf16(RIM, features)]
-        + [bf16(HD // 2, half)] * 3,
-        in_specs=[pl.BlockSpec(memory_space=pltpu.SMEM)] + [anywhere] * 3,
-        out_specs=[whole] * 5,
+        + [bf16(HD // 2, half)] * 3
+        + [jax.ShapeDtypeStruct(ids.shape, jnp.int32)],
+        in_specs=[pl.BlockSpec(memory_space=pltpu.SMEM)] + [far] * 5,
+        out_specs=[whole] * 6,
         scratch_shapes=[
             pltpu.VMEM(frames.shape, frames.dtype),
             pltpu.VMEM(taps.shape, taps.dtype),
-            pltpu.SemaphoreType.DMA((5,)),
+            pltpu.VMEM(ids.shape, ids.dtype),
+            pltpu.SMEM(owner.shape, owner.dtype),
+            pltpu.SemaphoreType.DMA((7,)),
         ],
-        compiler_params=pltpu.CompilerParams(vmem_limit_bytes=48 * 2**20),
+        compiler_params=pltpu.CompilerParams(vmem_limit_bytes=63 * 2**20),
         name="first",
-    )(scalars, frames, weight, taps)
+    )(scalars, owner, ids, frames, weight, taps)
 
 
 def early_kernel(rim, frames, taps, late, early, own):
@@ -268,27 +271,12 @@
     half = features // 2
     turn = lax.rem(2 * head + near, 3)
     turn_paired = lax.rem(2 * head + 1 - near, 3)
-    scalars = jnp.stack([me, near, grp, turn, turn_paired, head, devices])
+    scalars = jnp.stack([me, near, grp, turn, turn_paired, head])
     scalars = scalars.astype(jnp.int32)
 
-    codes = call(
-        code_kernel,
-        jax.ShapeDtypeStruct((1, tok_rows), jnp.int32),
-        [scalars, track_owner, track_ids[None, :]],
-        "code",
-        smem=2,
-        limit=1,
-    )
-    seen = [0]
-
-    def with_codes_of(codes, bit):
-        seen.extend([hop ^ bit for hop in seen])
-        return jnp.concatenate([codes, swap_seq(codes, bit)], axis=0)
-
-    codes = with_codes_of(with_codes_of(codes, FAR), NEAR)
-    late, rim_rows, *blocks = first(scalars, frames, qkv_weight.T, conv_weight)
-    late = after(late, codes)
-    rim_rows = after(rim_rows, codes)
+    late, rim_rows, *blocks, codes = first(
+        scalars, track_owner[None, :], track_ids[None, :], frames, qkv_weight.T, conv_weight
+    )
 
     def home(block):
         of_head, side = block % devices // 2, block % 2
@@ -301,6 +289,13 @@
         ]
     )
     far_late = swap_seq(late, FAR)
+    seen = [0]
+
+    def with_codes_of(codes, bit):
+        seen.extend([hop ^ bit for hop in seen])
+        return jnp.concatenate([codes, swap_seq(codes, bit)], axis=0)
+
+    codes = with_codes_of(codes, FAR)
     mine = after(mine, far_late)
     mine_too = swap_grp(mine)
     paired = swap_seq(mine, NEAR)
@@ -324,7 +319,7 @@
     beside = swap_seq(after(own, mine), Y)
     far_late_beside = swap_seq(far_late, Y)
     far_early = swap_seq(after(early, far_late), FAR)
-    far_early_beside = swap_seq(after(far_early, *diagonal), Y)
+    far_early_beside = swap_seq(after(far_early, codes, *diagonal), Y)
 
     parts = []
 
@@ -339,7 +334,7 @@
     done = project(own, beside, far_late, far_late_beside)
     done = project(far_early, after(far_early_beside, done))
 
-    codes = with_codes_of(with_codes_of(after(codes, done), CORE), Y)
+    codes = with_codes_of(with_codes_of(with_codes_of(after(codes, done), CORE), Y), NEAR)
 
     keyed = jnp.concatenate([p[1] for p in parts] + [p[2] for p in parts], axis=0)
 

time: 103 us -> 99.8 us (0.969)
  starting transfers between devices: 36.1 us -> 30.6 us
  Pallas kernels: 4.02 us -> 6.3 us
  local copies, waits for them, and re-layouts: 5.12 us -> 3.35 us
  waiting for transfers between devices: 49 us -> 50.5 us
    ppermute x3, waiting for transfers between devices: 7.15 us -> 11.1 us  [body_by_head(): lax.ppermute(block, FOUR, [(d, home(3 * d + j)) for d in range(devices)])]
    ppermute x23, starting transfers between devices: 24.4 us -> 21.1 us  [swap_seq(): return lax.ppermute(value, FOUR, [(d, d ^ bit) for d in range(count)])]
    ppermute x3, starting transfers between devices: 8.25 us -> 5.05 us  [body_by_head(): lax.ppermute(block, FOUR, [(d, home(3 * d + j)) for d in range(devices)])]
    ppermute x2, waiting for transfers between devices: 7.22 us -> 4.51 us  [swap_grp(): return lax.ppermute(value, 'grp', [(0, 1), (1, 0)])]
    unnamed x25 -> x23, local copies, waits for them, and re-layouts: 4.48 us -> 2.06 us
    pallas_call x1, Pallas kernels: 1.07 us -> 3.01 us  [first(): pl.pallas_call(first_kernel, out_shape=[bf16(tok_rows // 2, features), bf...]
    ppermute x1, starting transfers between devices: 1.29 us -> 2.36 us  [body_by_head(): lax.ppermute(rim_rows, FOUR, [(i, i + 1) for i in range(devices - 1)])]
    pallas_call x4 -> x3, Pallas kernels: 2.94 us -> 3.28 us  [call(): pl.pallas_call(kernel, out_shape=out_shape, in_specs=[scalars] * smem + [...]
  transfers between devices with their start and end apart: 29 -> 29, of which waited for: 17 -> 16; matrix products, arithmetic and copies ran while one was open for 6% -> 6% of each run, Pallas kernels for 2% -> 1%
where the time goes in v1:
time: 99.8 us; the launch traced here: 99.5 us
  waiting for transfers between devices  50.5 us (51%)
  starting transfers between devices  30.6 us (31%)
  matrix products  6.81 us (7%)
  Pallas kernels  6.3 us (6%)
  local copies, waits for them, and re-layouts  3.35 us (3%)
  other arithmetic  1.61 us (2%)
    ppermute x23, waiting for transfers between devices, swap_seq(): return lax.ppermute(value, FOUR, [(d, d ^ bit) for d in range(count)])  33.8 us
    ppermute x23, starting transfers between devices, swap_seq(): return lax.ppermute(value, FOUR, [(d, d ^ bit) for d in range(count)])  21.1 us
    ppermute x3, waiting for transfers between devices, body_by_head(): lax.ppermute(block, FOUR, [(d, home(3 * d + j)) for d in range(devices)])  11.1 us
    ppermute x3, starting transfers between devices, body_by_head(): lax.ppermute(block, FOUR, [(d, home(3 * d + j)) for d in range(devices)])  5.05 us
    ppermute x2, waiting for transfers between devices, swap_grp(): return lax.ppermute(value, 'grp', [(0, 1), (1, 0)])  4.51 us
    pallas_call x3, Pallas kernels, call(): pl.pallas_call(kernel, out_shape=out_shape, in_specs=[scalars] * smem + [...  3.28 us
    pallas_call x1, Pallas kernels, first(): pl.pallas_call(first_kernel, out_shape=[bf16(tok_rows // 2, features), bf...  3.01 us
    dot_general x2, matrix products, attend(): lax.dot_general(query, keyed[:, :HD], (((1,), (1,)), ((), ())), preferred...  2.53 us
  transfers between devices with their start and end apart: 29, of which 16 were waited for; matrix products, arithmetic and copies ran while one was open for 6% of the time, Pallas kernels for 1%

profile of v1, /device:TPU:0, one launch (start us, length us, event | category | flops | bytes accessed | tf_op | source)
XLA Modules:
  0.0 99.5 jit_solution(12173919097019521996)
XLA Ops:
  0.7 3.0 %first.1 = (bf16[64,2048]{1,0:T(8,128)(2,1)}, bf16[16,2048]{1,0:T(8,128)(2,1)}, bf16[64,1024]{1,0:T(8,128)(2,1)}, bf16[64,1024]{1,0:T(8,128)(2,1)}, bf16[64,1024]{1,0:T(8,128)(2,1)}, /*index=5*/s32[1,128]{1,0:T(1,128)}) custom-call(s32[6]{0:T(128)} %stack.39.scalars, s32[1,64]{1,0:T(1,128)} %bitcast.86, s32[1,128]{1,0:T(1,128)} %bitcast.87, ...), custom_call_target="tpu_custom_call" | custom-call | tf_op jit(solution)/shard_map/first/pallas_call | solution.py:210
  3.7 2.4 %collective-permute-start.1 = (bf16[16,2048]{1,0:T(8,128)(2,1)}, bf16[16,2048]{1,0:T(8,128)(2,1)S(1)}, u32[]{:S(2)}, u32[]{:S(2)}) collective-permute-start(bf16[16,2048]{1,0:T(8,128)(2,1)} %get-tuple-element.14), channel_id=1, source_target_pairs={{0,1},{1,2},{2,3},{3,4},{4,5},{5,6},{6,7},{7,8},{8,9},{9,10},{10,1... | collective-permute-start | bytes 196616 | tf_op jit(solution)/shard_map/ppermute | solution.py:312
  10.2 3.2 %collective-permute-start.14 = (bf16[128,2048]{1,0:T(8,128)(2,1)S(1)}, bf16[128,2048]{1,0:T(8,128)(2,1)S(1)}, u32[]{:S(2)}, u32[]{:S(2)}) collective-permute-start(bf16[128,2048]{1,0:T(8,128)(2,1)S(1)} %get-tuple-element.20.refs_0_), channel_id=1, source_target_pairs={{0,1},{1,0},{2,3},{3,2},{4,5},{5,4},{6,7},{7,6},{8,9},{9,8},{10,11... | collective-permute-start | bytes 1572872 | tf_op jit(solution)/shard_map/ppermute | solution.py:112
  13.5 4.2 %collective-permute-start.2 = (bf16[64,2048]{1,0:T(8,128)(2,1)}, bf16[64,2048]{1,0:T(8,128)(2,1)S(1)}, u32[]{:S(2)}, u32[]{:S(2)}) collective-permute-start(bf16[64,2048]{1,0:T(8,128)(2,1)} %get-tuple-element.15.late), channel_id=1, source_target_pairs={{0,8},{1,9},{2,10},{3,11},{4,12},{5,13},{6,14},{7,15},{8,0},{9,1},... | collective-permute-start | bytes 786440 | tf_op jit(solution)/shard_map/ppermute | solution.py:112
  17.6 1.6 %collective-permute-start.5 = (bf16[64,1024]{1,0:T(8,128)(2,1)}, bf16[64,1024]{1,0:T(8,128)(2,1)S(1)}, u32[]{:S(2)}, u32[]{:S(2)}) collective-permute-start(bf16[64,1024]{1,0:T(8,128)(2,1)} %get-tuple-element.18), channel_id=1, source_target_pairs={{0,4},{1,2},{2,7},{3,9},{4,14},{5,0},{6,5},{7,3},{8,12},{9,10},{10... | collective-permute-start | bytes 393224 | tf_op jit(solution)/shard_map/ppermute | solution.py:287
  19.2 1.9 %collective-permute-start.6 = (bf16[64,1024]{1,0:T(8,128)(2,1)}, bf16[64,1024]{1,0:T(8,128)(2,1)S(1)}, u32[]{:S(2)}, u32[]{:S(2)}) collective-permute-start(bf16[64,1024]{1,0:T(8,128)(2,1)} %get-tuple-element.19), channel_id=1, source_target_pairs={{0,1},{1,6},{2,8},{3,13},{4,11},{5,4},{6,2},{7,7},{8,9},{9,14},{10... | collective-permute-start | bytes 393224 | tf_op jit(solution)/shard_map/ppermute | solution.py:287
  21.1 1.6 %collective-permute-start.4 = (bf16[64,1024]{1,0:T(8,128)(2,1)}, bf16[64,1024]{1,0:T(8,128)(2,1)S(1)}, u32[]{:S(2)}, u32[]{:S(2)}) collective-permute-start(bf16[64,1024]{1,0:T(8,128)(2,1)} %get-tuple-element.17), channel_id=1, source_target_pairs={{0,0},{1,5},{2,3},{3,12},{4,10},{5,15},{6,1},{7,6},{8,8},{9,13},{1... | collective-permute-start | bytes 393224 | tf_op jit(solution)/shard_map/ppermute | solution.py:287
  22.7 4.7 %collective-permute-done.5 = bf16[64,1024]{1,0:T(8,128)(2,1)S(1)} collective-permute-done((bf16[64,1024]{1,0:T(8,128)(2,1)}, bf16[64,1024]{1,0:T(8,128)(2,1)S(1)}, u32[]{:S(2)}, u32[]{:S(2)}) %collective-permute-start.5) | collective-permute-done | bytes 131104 | tf_op jit(solution)/shard_map/ppermute | solution.py:287
  27.4 6.4 %collective-permute-done.6 = bf16[64,1024]{1,0:T(8,128)(2,1)S(1)} collective-permute-done((bf16[64,1024]{1,0:T(8,128)(2,1)}, bf16[64,1024]{1,0:T(8,128)(2,1)S(1)}, u32[]{:S(2)}, u32[]{:S(2)}) %collective-permute-start.6) | collective-permute-done | bytes 131104 | tf_op jit(solution)/shard_map/ppermute | solution.py:287
  33.9 2.1 %collective-permute-done.2.refs_1_ = bf16[64,2048]{1,0:T(8,128)(2,1)S(1)} collective-permute-done((bf16[64,2048]{1,0:T(8,128)(2,1)}, bf16[64,2048]{1,0:T(8,128)(2,1)S(1)}, u32[]{:S(2)}, u32[]{:S(2)}) %collective-permute-start.2) | collective-permute-done | bytes 262176 | tf_op jit(solution)/shard_map/ppermute | solution.py:112
  36.0 1.5 %collective-permute-start.9 = (bf16[3,64,1024]{2,1,0:T(8,128)(2,1)S(1)}, bf16[3,64,1024]{2,1,0:T(8,128)(2,1)S(1)}, u32[]{:S(2)}, u32[]{:S(2)}) collective-permute-start(bf16[3,64,1024]{2,1,0:T(8,128)(2,1)S(1)} %after.7.refs_1_.mine), channel_id=1, source_target_pairs={{0,16},{16,0},{1,17},{17,1},{2,18},{18,2},{3,19},{19,3},{4,20},{20... | collective-permute-start | bytes 1179656 | tf_op jit(solution)/shard_map/ppermute | solution.py:116
  39.1 3.3 %collective-permute-start.3 = (bf16[64,2048]{1,0:T(8,128)(2,1)S(1)}, bf16[64,2048]{1,0:T(8,128)(2,1)S(1)}, u32[]{:S(2)}, u32[]{:S(2)}) collective-permute-start(bf16[64,2048]{1,0:T(8,128)(2,1)S(1)} %after.6), channel_id=1, source_target_pairs={{0,8},{1,9},{2,10},{3,11},{4,12},{5,13},{6,14},{7,15},{8,0},{9,1},... | collective-permute-start | bytes 786440 | tf_op jit(solution)/shard_map/ppermute | solution.py:112
  42.4 4.4 %collective-permute-done.9.mine_too = bf16[3,64,1024]{2,1,0:T(8,128)(2,1)S(1)} collective-permute-done((bf16[3,64,1024]{2,1,0:T(8,128)(2,1)S(1)}, bf16[3,64,1024]{2,1,0:T(8,128)(2,1)S(1)}, u32[]{:S(2)}, u32[]{:S(2)}) %collective-permute-start.9) | collective-permute-done | bytes 393248 | tf_op jit(solution)/shard_map/ppermute | solution.py:116
  47.6 6.1 %collective-permute-done.7.paired = bf16[3,64,1024]{2,1,0:T(8,128)(2,1)S(1)} collective-permute-done((bf16[3,64,1024]{2,1,0:T(8,128)(2,1)S(1)}, bf16[3,64,1024]{2,1,0:T(8,128)(2,1)S(1)}, u32[]{:S(2)}, u32[]{:S(2)}) %collective-permute-start.7) | collective-permute-done | bytes 393248 | tf_op jit(solution)/shard_map/ppermute | solution.py:112
  54.5 2.2 %collective-permute-done.13 = bf16[64,2048]{1,0:T(8,128)(2,1)S(1)} collective-permute-done((bf16[64,2048]{1,0:T(8,128)(2,1)S(1)}, bf16[64,2048]{1,0:T(8,128)(2,1)S(1)}, u32[]{:S(2)}, u32[]{:S(2)}) %collective-permute-start.13) | collective-permute-done | bytes 262176 | tf_op jit(solution)/shard_map/ppermute | solution.py:112
  56.6 2.7 %collective-permute-done.10.refs_3_.diagonal1 = bf16[3,64,512]{2,1,0:T(8,128)(2,1)S(1)} collective-permute-done((bf16[3,64,512]{2,1,0:T(8,128)(2,1)S(1)}, bf16[3,64,512]{2,1,0:T(8,128)(2,1)S(1)}, u32[]{:S(2)}, u32[]{:S(2)}) %collective-permute-start.10) | collective-permute-done | bytes 196640 | tf_op jit(solution)/shard_map/ppermute | solution.py:112
  60.8 1.7 %collective-permute-done.15 = bf16[128,2048]{1,0:T(8,128)(2,1)S(1)} collective-permute-done((bf16[128,2048]{1,0:T(8,128)(2,1)S(1)}, bf16[128,2048]{1,0:T(8,128)(2,1)S(1)}, u32[]{:S(2)}, u32[]{:S(2)}) %collective-permute-start.15) | collective-permute-done | bytes 524320 | tf_op jit(solution)/shard_map/ppermute | solution.py:112
  62.6 1.8 %convolution_convert_fusion.refs_1_ = bf16[768,384]{1,0:T(8,128)(2,1)S(1)} fusion(bf16[768,2048]{1,0:T(8,128)(2,1)S(1)} %constant_dynamic-update-slice_fusion, bf16[384,2048]{1,0:T(8,128)(2,1)S(1)} %assemble.1), kind=kOutput, calls=%fused_computation.10 | convolution fusion | flops 1208254464 | bytes 5308416 | tf_op jit(solution)/shard_map/dot_general | solution.py:328
  64.4 3.7 %collective-permute-done.11.refs_0_ = bf16[64,2048]{1,0:T(8,128)(2,1)S(1)} collective-permute-done((bf16[64,2048]{1,0:T(8,128)(2,1)S(1)}, bf16[64,2048]{1,0:T(8,128)(2,1)S(1)}, u32[]{:S(2)}, u32[]{:S(2)}) %collective-permute-start.11) | collective-permute-done | bytes 262176 | tf_op jit(solution)/shard_map/ppermute | solution.py:112
  72.0 3.2 %collective-permute-done.21 = s32[4,128]{1,0:T(4,128)S(1)} collective-permute-done((s32[4,128]{1,0:T(4,128)S(1)}, s32[4,128]{1,0:T(4,128)S(1)}, u32[]{:S(2)}, u32[]{:S(2)}) %collective-permute-start.21) | collective-permute-done | bytes 2080 | tf_op jit(solution)/shard_map/ppermute | solution.py:112
  76.8 5.8 %collective-permute-done.22 = s32[8,128]{1,0:T(8,128)S(1)} collective-permute-done((s32[8,128]{1,0:T(8,128)S(1)}, s32[8,128]{1,0:T(8,128)S(1)}, u32[]{:S(2)}, u32[]{:S(2)}) %collective-permute-start.22) | collective-permute-done | bytes 4128 | tf_op jit(solution)/shard_map/ppermute | solution.py:112
  85.8 1.6 %collective-permute-start.26 = (bf16[2,128,128]{2,1,0:T(8,128)(2,1)S(1)}, bf16[2,128,128]{2,1,0:T(8,128)(2,1)S(1)}, u32[]{:S(2)}, u32[]{:S(2)}) collective-permute-start(bf16[2,128,128]{2,1,0:T(8,128)(2,1)S(1)} %bitcast.85), channel_id=1, source_target_pairs={{0,8},{1,9},{2,10},{3,11},{4,12},{5,13},{6,14},{7,15},{8,0},{9,1},... | collective-permute-start | bytes 196616 | tf_op jit(solution)/shard_map/ppermute | solution.py:112
  91.5 1.7 %collective-permute-start.25 = (bf16[2,128,128]{2,1,0:T(8,128)(2,1)S(1)}, bf16[2,128,128]{2,1,0:T(8,128)(2,1)S(1)}, u32[]{:S(2)}, u32[]{:S(2)}) collective-permute-start(bf16[2,128,128]{2,1,0:T(8,128)(2,1)S(1)} %bitcast.83), channel_id=1, source_target_pairs={{0,2},{1,3},{2,0},{3,1},{4,6},{5,7},{6,4},{7,5},{8,10},{9,11},{10,... | collective-permute-start | bytes 196616 | tf_op jit(solution)/shard_map/ppermute | solution.py:112
  93.2 3.5 %collective-permute-done.27 = bf16[2,128,128]{2,1,0:T(8,128)(2,1)S(1)} collective-permute-done((bf16[2,128,128]{2,1,0:T(8,128)(2,1)S(1)}, bf16[2,128,128]{2,1,0:T(8,128)(2,1)S(1)}, u32[]{:S(2)}, u32[]{:S(2)}) %collective-permute-start.27) | collective-permute-done | bytes 65568 | tf_op jit(solution)/shard_map/ppermute | solution.py:112
  (107 shorter events, 24.9 us)
Async XLA Ops:
  3.7 3.5 %collective-permute-start.1 = (bf16[16,2048]{1,0:T(8,128)(2,1)}, bf16[16,2048]{1,0:T(8,128)(2,1)S(1)}, u32[]{:S(2)}, u32[]{:S(2)}) collective-permute-start(bf16[16,2048]{1,0:T(8,128)(2,1)} %get-tuple-element.14), channel_id=1, source_target_pairs={{0,1},{1,2},{2,3},{3,4},{4,5},{5,6},{6,7},{7,8},{8,9},{9,10},{10,1... | collective-permute-start | bytes 196616 | tf_op jit(solution)/shard_map/ppermute | solution.py:312
  10.2 28.3 %collective-permute-start.14 = (bf16[128,2048]{1,0:T(8,128)(2,1)S(1)}, bf16[128,2048]{1,0:T(8,128)(2,1)S(1)}, u32[]{:S(2)}, u32[]{:S(2)}) collective-permute-start(bf16[128,2048]{1,0:T(8,128)(2,1)S(1)} %get-tuple-element.20.refs_0_), channel_id=1, source_target_pairs={{0,1},{1,0},{2,3},{3,2},{4,5},{5,4},{6,7},{7,6},{8,9},{9,8},{10,11... | collective-permute-start | bytes 1572872 | tf_op jit(solution)/shard_map/ppermute | solution.py:112
  13.5 22.5 %collective-permute-start.2 = (bf16[64,2048]{1,0:T(8,128)(2,1)}, bf16[64,2048]{1,0:T(8,128)(2,1)S(1)}, u32[]{:S(2)}, u32[]{:S(2)}) collective-permute-start(bf16[64,2048]{1,0:T(8,128)(2,1)} %get-tuple-element.15.late), channel_id=1, source_target_pairs={{0,8},{1,9},{2,10},{3,11},{4,12},{5,13},{6,14},{7,15},{8,0},{9,1},... | collective-permute-start | bytes 786440 | tf_op jit(solution)/shard_map/ppermute | solution.py:112
  17.6 9.8 %collective-permute-start.5 = (bf16[64,1024]{1,0:T(8,128)(2,1)}, bf16[64,1024]{1,0:T(8,128)(2,1)S(1)}, u32[]{:S(2)}, u32[]{:S(2)}) collective-permute-start(bf16[64,1024]{1,0:T(8,128)(2,1)} %get-tuple-element.18), channel_id=1, source_target_pairs={{0,4},{1,2},{2,7},{3,9},{4,14},{5,0},{6,5},{7,3},{8,12},{9,10},{10... | collective-permute-start | bytes 393224 | tf_op jit(solution)/shard_map/ppermute | solution.py:287
  19.2 14.6 %collective-permute-start.6 = (bf16[64,1024]{1,0:T(8,128)(2,1)}, bf16[64,1024]{1,0:T(8,128)(2,1)S(1)}, u32[]{:S(2)}, u32[]{:S(2)}) collective-permute-start(bf16[64,1024]{1,0:T(8,128)(2,1)} %get-tuple-element.19), channel_id=1, source_target_pairs={{0,1},{1,6},{2,8},{3,13},{4,11},{5,4},{6,2},{7,7},{8,9},{9,14},{10... | collective-permute-start | bytes 393224 | tf_op jit(solution)/shard_map/ppermute | solution.py:287
  21.1 12.7 %collective-permute-start.4 = (bf16[64,1024]{1,0:T(8,128)(2,1)}, bf16[64,1024]{1,0:T(8,128)(2,1)S(1)}, u32[]{:S(2)}, u32[]{:S(2)}) collective-permute-start(bf16[64,1024]{1,0:T(8,128)(2,1)} %get-tuple-element.17), channel_id=1, source_target_pairs={{0,0},{1,5},{2,3},{3,12},{4,10},{5,15},{6,1},{7,6},{8,8},{9,13},{1... | collective-permute-start | bytes 393224 | tf_op jit(solution)/shard_map/ppermute | solution.py:287
  36.0 10.9 %collective-permute-start.9 = (bf16[3,64,1024]{2,1,0:T(8,128)(2,1)S(1)}, bf16[3,64,1024]{2,1,0:T(8,128)(2,1)S(1)}, u32[]{:S(2)}, u32[]{:S(2)}) collective-permute-start(bf16[3,64,1024]{2,1,0:T(8,128)(2,1)S(1)} %after.7.refs_1_.mine), channel_id=1, source_target_pairs={{0,16},{16,0},{1,17},{17,1},{2,18},{18,2},{3,19},{19,3},{4,20},{20... | collective-permute-start | bytes 1179656 | tf_op jit(solution)/shard_map/ppermute | solution.py:116
  37.5 16.2 %collective-permute-start.7 = (bf16[3,64,1024]{2,1,0:T(8,128)(2,1)S(1)}, bf16[3,64,1024]{2,1,0:T(8,128)(2,1)S(1)}, u32[]{:S(2)}, u32[]{:S(2)}) collective-permute-start(bf16[3,64,1024]{2,1,0:T(8,128)(2,1)S(1)} %after.7.refs_1_.mine), channel_id=1, source_target_pairs={{0,4},{1,5},{2,6},{3,7},{4,0},{5,1},{6,2},{7,3},{8,12},{9,13},{10,... | collective-permute-start | bytes 1179656 | tf_op jit(solution)/shard_map/ppermute | solution.py:112
  38.6 21.9 %collective-permute-start.12 = (bf16[128,2048]{1,0:T(8,128)(2,1)S(1)}, bf16[128,2048]{1,0:T(8,128)(2,1)S(1)}, u32[]{:S(2)}, u32[]{:S(2)}) collective-permute-start(bf16[128,2048]{1,0:T(8,128)(2,1)S(1)} %after.9), channel_id=1, source_target_pairs={{0,2},{1,3},{2,0},{3,1},{4,6},{5,7},{6,4},{7,5},{8,10},{9,11},{10,... | collective-permute-start | bytes 1572872 | tf_op jit(solution)/shard_map/ppermute | solution.py:112
  39.1 15.3 %collective-permute-start.3 = (bf16[64,2048]{1,0:T(8,128)(2,1)S(1)}, bf16[64,2048]{1,0:T(8,128)(2,1)S(1)}, u32[]{:S(2)}, u32[]{:S(2)}) collective-permute-start(bf16[64,2048]{1,0:T(8,128)(2,1)S(1)} %after.6), channel_id=1, source_target_pairs={{0,8},{1,9},{2,10},{3,11},{4,12},{5,13},{6,14},{7,15},{8,0},{9,1},... | collective-permute-start | bytes 786440 | tf_op jit(solution)/shard_map/ppermute | solution.py:112
  42.4 14.3 %collective-permute-start.13 = (bf16[64,2048]{1,0:T(8,128)(2,1)S(1)}, bf16[64,2048]{1,0:T(8,128)(2,1)S(1)}, u32[]{:S(2)}, u32[]{:S(2)}) collective-permute-start(bf16[64,2048]{1,0:T(8,128)(2,1)S(1)} %collective-permute-done.2.refs_1_), channel_id=1, source_target_pairs={{0,2},{1,3},{2,0},{3,1},{4,6},{5,7},{6,4},{7,5},{8,10},{9,11},{10,... | collective-permute-start | bytes 786440 | tf_op jit(solution)/shard_map/ppermute | solution.py:112
  46.9 6.9 %collective-permute-start = (s32[1,128]{1,0:T(1,128)S(1)}, s32[1,128]{1,0:T(1,128)S(1)}, u32[]{:S(2)}, u32[]{:S(2)}) collective-permute-start(s32[1,128]{1,0:T(1,128)S(1)} %copy-done.3), channel_id=1, source_target_pairs={{0,8},{1,9},{2,10},{3,11},{4,12},{5,13},{6,14},{7,15},{8,0},{9,1},... | collective-permute-start | bytes 1544 | tf_op jit(solution)/shard_map/ppermute | solution.py:112
  53.7 5.7 %collective-permute-start.10 = (bf16[3,64,512]{2,1,0:T(8,128)(2,1)S(1)}, bf16[3,64,512]{2,1,0:T(8,128)(2,1)S(1)}, u32[]{:S(2)}, u32[]{:S(2)}) collective-permute-start(bf16[3,64,512]{2,1,0:T(8,128)(2,1)S(1)} %slice.261), channel_id=1, source_target_pairs={{0,4},{1,5},{2,6},{3,7},{4,0},{5,1},{6,2},{7,3},{8,12},{9,13},{10,... | collective-permute-start | bytes 589832 | tf_op jit(solution)/shard_map/ppermute | solution.py:112
  53.7 5.7 %collective-permute-start.8 = (bf16[3,64,512]{2,1,0:T(8,128)(2,1)S(1)}, bf16[3,64,512]{2,1,0:T(8,128)(2,1)S(1)}, u32[]{:S(2)}, u32[]{:S(2)}) collective-permute-start(bf16[3,64,512]{2,1,0:T(8,128)(2,1)S(1)} %slice.260), channel_id=1, source_target_pairs={{0,16},{16,0},{1,17},{17,1},{2,18},{18,2},{3,19},{19,3},{4,20},{20... | collective-permute-start | bytes 589832 | tf_op jit(solution)/shard_map/ppermute | solution.py:116
  54.3 8.2 %collective-permute-start.16 = (bf16[64,2048]{1,0:T(8,128)(2,1)S(1)}, bf16[64,2048]{1,0:T(8,128)(2,1)S(1)}, u32[]{:S(2)}, u32[]{:S(2)}) collective-permute-start(bf16[64,2048]{1,0:T(8,128)(2,1)S(1)} %collective-permute-done.2.refs_1_), channel_id=1, source_target_pairs={{0,1},{1,0},{2,3},{3,2},{4,5},{5,4},{6,7},{7,6},{8,9},{9,8},{10,11... | collective-permute-start | bytes 786440 | tf_op jit(solution)/shard_map/ppermute | solution.py:112
  56.6 11.7 %collective-permute-start.18 = (bf16[64,2048]{1,0:T(8,128)(2,1)S(1)}, bf16[64,2048]{1,0:T(8,128)(2,1)S(1)}, u32[]{:S(2)}, u32[]{:S(2)}) collective-permute-start(bf16[64,2048]{1,0:T(8,128)(2,1)S(1)} %collective-permute-done.3), channel_id=1, source_target_pairs={{0,1},{1,0},{2,3},{3,2},{4,5},{5,4},{6,7},{7,6},{8,9},{9,8},{10,11... | collective-permute-start | bytes 786440 | tf_op jit(solution)/shard_map/ppermute | solution.py:112
  59.5 8.6 %collective-permute-start.11 = (bf16[64,2048]{1,0:T(8,128)(2,1)S(1)}, bf16[64,2048]{1,0:T(8,128)(2,1)S(1)}, u32[]{:S(2)}, u32[]{:S(2)}) collective-permute-start(bf16[64,2048]{1,0:T(8,128)(2,1)S(1)} %after.8), channel_id=1, source_target_pairs={{0,2},{1,3},{2,0},{3,1},{4,6},{5,7},{6,4},{7,5},{8,10},{9,11},{10,... | collective-permute-start | bytes 786440 | tf_op jit(solution)/shard_map/ppermute | solution.py:112
  68.1 14.7 %collective-permute-start.23 = (bf16[768,256]{1,0:T(8,128)(2,1)S(1)}, bf16[768,256]{1,0:T(8,128)(2,1)S(1)}, u32[]{:S(2)}, u32[]{:S(2)}) collective-permute-start(bf16[768,256]{1,0:T(8,128)(2,1)S(1)} %slice.266), channel_id=1, source_target_pairs={{0,4},{1,5},{2,6},{3,7},{4,0},{5,1},{6,2},{7,3},{8,12},{9,13},{10,... | collective-permute-start | bytes 1179656 | tf_op jit(solution)/shard_map/ppermute | solution.py:112
  70.8 12.0 %collective-permute-start.24 = (bf16[256,256]{1,0:T(8,128)(2,1)S(1)}, bf16[256,256]{1,0:T(8,128)(2,1)S(1)}, u32[]{:S(2)}, u32[]{:S(2)}) collective-permute-start(bf16[256,256]{1,0:T(8,128)(2,1)S(1)} %slice.267), channel_id=1, source_target_pairs={{0,4},{1,5},{2,6},{3,7},{4,0},{5,1},{6,2},{7,3},{8,12},{9,13},{10,... | collective-permute-start | bytes 393224 | tf_op jit(solution)/shard_map/ppermute | solution.py:112
  71.6 3.6 %collective-permute-start.21 = (s32[4,128]{1,0:T(4,128)S(1)}, s32[4,128]{1,0:T(4,128)S(1)}, u32[]{:S(2)}, u32[]{:S(2)}) collective-permute-start(s32[4,128]{1,0:T(4,128)S(1)} %pad_add_fusion.1), channel_id=1, source_target_pairs={{0,2},{1,3},{2,0},{3,1},{4,6},{5,7},{6,4},{7,5},{8,10},{9,11},{10,... | collective-permute-start | bytes 6152 | tf_op jit(solution)/shard_map/ppermute | solution.py:112
  75.4 7.2 %collective-permute-start.22 = (s32[8,128]{1,0:T(8,128)S(1)}, s32[8,128]{1,0:T(8,128)S(1)}, u32[]{:S(2)}, u32[]{:S(2)}) collective-permute-start(s32[8,128]{1,0:T(8,128)S(1)} %pad_add_fusion), channel_id=1, source_target_pairs={{0,4},{1,5},{2,6},{3,7},{4,0},{5,1},{6,2},{7,3},{8,12},{9,13},{10,... | collective-permute-start | bytes 12296 | tf_op jit(solution)/shard_map/ppermute | solution.py:112
  85.8 7.4 %collective-permute-start.26 = (bf16[2,128,128]{2,1,0:T(8,128)(2,1)S(1)}, bf16[2,128,128]{2,1,0:T(8,128)(2,1)S(1)}, u32[]{:S(2)}, u32[]{:S(2)}) collective-permute-start(bf16[2,128,128]{2,1,0:T(8,128)(2,1)S(1)} %bitcast.85), channel_id=1, source_target_pairs={{0,8},{1,9},{2,10},{3,11},{4,12},{5,13},{6,14},{7,15},{8,0},{9,1},... | collective-permute-start | bytes 196616 | tf_op jit(solution)/shard_map/ppermute | solution.py:112
  90.2 6.5 %collective-permute-start.27 = (bf16[2,128,128]{2,1,0:T(8,128)(2,1)S(1)}, bf16[2,128,128]{2,1,0:T(8,128)(2,1)S(1)}, u32[]{:S(2)}, u32[]{:S(2)}) collective-permute-start(bf16[2,128,128]{2,1,0:T(8,128)(2,1)S(1)} %bitcast.84), channel_id=1, source_target_pairs={{0,10},{1,11},{2,8},{3,9},{4,14},{5,15},{6,12},{7,13},{8,2},{9,3},... | collective-permute-start | bytes 196616 | tf_op jit(solution)/shard_map/ppermute | solution.py:112
  91.5 5.2 %collective-permute-start.25 = (bf16[2,128,128]{2,1,0:T(8,128)(2,1)S(1)}, bf16[2,128,128]{2,1,0:T(8,128)(2,1)S(1)}, u32[]{:S(2)}, u32[]{:S(2)}) collective-permute-start(bf16[2,128,128]{2,1,0:T(8,128)(2,1)S(1)} %bitcast.83), channel_id=1, source_target_pairs={{0,2},{1,3},{2,0},{3,1},{4,6},{5,7},{6,4},{7,5},{8,10},{9,11},{10,... | collective-permute-start | bytes 196616 | tf_op jit(solution)/shard_map/ppermute | solution.py:112
  (9 other events, 80.2 us)
